TPU v7x, 32 devices: a whole 2x2x4 slice. The times are simulated.
32 devices in a mesh: redist: 8 (over y, x, core), rep: 4 (over z).
Axes of the slice: x: 2, y: 2, z: 4, core: 2. Of those that a mesh axis runs over, the one named last changes fastest.
Arguments:
- amplitudes: bfloat16 [4, 128, 1024, 1024], P(None, ('redist', 'rep')), may hold values from -6 to 6
- integrals: bfloat16 [128, 1024, 2, 1024], P(None, 'redist'), may hold values from -0.046875 to 0.046875
- occ_irrep: int32 [128], replicated, may hold values from 0 to 7, as said below
- virt_irrep: int32 [1024], replicated, may hold values from 0 to 7, as said below
Outputs:
- cycle_term: float32 [4, 1024, 2, 1024], P(None, None, None, 'redist')
Inputs may be any that keep to these rules, and one draw needn't show every extreme that they name: `occ_irrep`: labels never fall along the orbitals; each of the 8 irreps holds one contiguous range of between n // 16 and 3 * n // 16 orbitals, n being 128 or 1024. `virt_irrep`: labels never fall along the orbitals; each of the 8 irreps holds one contiguous range of between n // 16 and 3 * n // 16 orbitals, n being 128 or 1024.
All inputs are finite; a program needn't handle non-finite values.
Results may differ from a plain program's by a relative error of at most 0.0003.
Values may be sent and summed in bfloat16 or wider, within the bound.
A program may use at most 256 MiB of HBM per device.

v0:
```python
import jax
import jax.numpy as jnp
from jax import lax
from jax.sharding import PartitionSpec as P


def irrep_allowed(occ_rows, occ_cols, virt_rows, virt_cols):
    pair_ik = jnp.bitwise_xor(occ_rows[:, None], occ_cols[None, :])
    pair_ac = jnp.bitwise_xor(virt_rows[:, None], virt_cols[None, :])
    return pair_ik[:, :, None, None] == pair_ac[None, None, :, :]


def integral_allowed(occ_ks, virt_cs, occ_js, virt_bs):
    pair_kc = jnp.bitwise_xor(occ_ks[:, None], virt_cs[None, :])
    pair_jb = jnp.bitwise_xor(occ_js[:, None], virt_bs[None, :])
    return pair_kc[:, :, None, None] == pair_jb[None, None, :, :]


def contract(masked, operand):
    return lax.dot_general(
        masked, operand, (((1, 3), (0, 1)), ((), ())), preferred_element_type=jnp.float32
    )


def body(amplitudes, integrals, occ_irrep, virt_irrep):
    n_redist = lax.axis_size("redist")
    n_rep = lax.axis_size("rep")
    dev_index = lax.axis_index("redist")
    rep_index = lax.axis_index("rep")
    i_slab, k_block, v_width, _ = amplitudes.shape
    c_block = integrals.shape[1]
    j_slab = integrals.shape[2]
    occ_rows = occ_irrep[:i_slab]
    occ_js = occ_irrep[:j_slab]
    zero_value = jnp.zeros((), amplitudes.dtype)
    grouped_ints = integrals.reshape(n_redist, n_rep, k_block, c_block, j_slab, v_width)
    ints_mine = lax.dynamic_slice_in_dim(grouped_ints, rep_index, 1, 1).reshape(
        n_redist * k_block, c_block, j_slab, v_width
    )
    moved = lax.all_to_all(ints_mine, "redist", split_axis=0, concat_axis=1, tiled=True)
    occ_cols = lax.dynamic_slice_in_dim(
        occ_irrep, (dev_index * n_rep + rep_index) * k_block, k_block
    )
    masked = jnp.where(
        irrep_allowed(occ_rows, occ_cols, virt_irrep, virt_irrep), amplitudes, zero_value
    )
    sym_ints = jnp.where(
        integral_allowed(occ_cols, virt_irrep, occ_js, virt_irrep), moved, zero_value
    )
    partial_value = contract(masked, sym_ints)
    shares = lax.psum_scatter(partial_value, "redist", scatter_dimension=3, tiled=True)
    return lax.psum(shares, "rep")


def solution(mesh):
    placed = (P(None, ("redist", "rep"), None, None), P(None, "redist", None, None), P(), P())
    return jax.shard_map(
        body, mesh=mesh, in_specs=placed, out_specs=P(None, None, None, "redist"), check_vma=False
    )
```

profile of v0, /device:TPU:0, one launch (start us, length us, event | category | flops | bytes accessed | tf_op | source)
XLA Modules:
  0.0 692.6 jit_solution(17488066635338278296)
XLA Ops:
  6.5 13.3 %constant_dynamic-slice_fusion = bf16[8,1,4,128,2,1024]{5,4,3,2,1,0:T(2,128)(2,1)S(1)} fusion(bf16[8,4,4,128,2,1024]{5,4,3,2,1,0:T(2,128)(2,1)} %bitcast.2, s32[]{:T(128)S(6)} %select_n.16), kind=kLoop, calls=%fused_computation.14 | loop fusion | bytes 33554436 | tf_op jit(solution)/shard_map/dynamic_slice | solution.py:37
  19.9 8.8 %copy.14 = bf16[8,1,4,128,2,1024]{5,3,4,2,0,1:T(8,128)(2,1)} copy(bf16[8,1,4,128,2,1024]{5,4,3,2,1,0:T(2,128)(2,1)S(1)} %constant_dynamic-slice_fusion) | data formatting | bytes 33554432
  28.6 0.0 copy-start.1
  28.6 0.0 copy-start
  28.6 5.9 all-to-all-start
  34.5 0.0 reduce-scatter.2.cloned.1.call-start
  34.6 0.0 copy-done.1
  34.6 0.1 fusion.14
  34.7 0.1 broadcast_xor_fusion.3
  34.7 0.0 copy-done
  34.7 0.1 broadcast_xor_fusion.2
  34.8 0.1 broadcast_xor_fusion.1
  34.9 2.4 broadcast_xor_fusion
  37.2 181.9 %all-to-all-done = bf16[32,128,2,1024]{3,1,2,0:T(8,128)(2,1)} async-done(((bf16[32,128,2,1024]{3,1,2,0:T(8,128)(2,1)}), bf16[32,128,2,1024]{3,1,2,0:T(8,128)(2,1)}, u32[]{:S(2)}, u32[]{:S(2)}) %all-to-all-start) | async-done | bytes 16777248 | tf_op jit(solution)/shard_map/all_to_all | solution.py:40
  219.1 8.5 %copy.9 = bf16[4,8,128,2,1024]{4,2,1,3,0:T(8,128)(2,1)S(1)} copy(bf16[4,8,128,2,1024]{4,2,3,0,1:T(8,128)(2,1)} %bitcast.5) | data formatting | bytes 33554432 | tf_op jit(solution)/shard_map/all_to_all | solution.py:40
  227.6 8.6 %compare_select_fusion.1 = bf16[4,1024,2,1024]{3,1,2,0:T(8,128)(2,1)} fusion(bf16[4,8,128,2,1024]{4,2,1,3,0:T(8,128)(2,1)S(1)} %copy.9, s32[2,1024]{1,0:T(2,128)S(1)} %broadcast_xor_fusion.2, s32[4,1024]{1,0:T(4,128)S(1)} %broadcast_xor_fusion.1), kind=kLoop, calls=%fused_computation.5 | loop fusion | flops 16777216 | bytes 33579008 | tf_op jit(solution)/shard_map/jit(_where)/select_n | solution.py:47
  236.2 79.0 %fusion.8 = f32[4,1024,2,1024]{3,1,2,0:T(8,128)} fusion(bf16[4,1024,2,1024]{3,1,2,0:T(8,128)(2,1)} %compare_select_fusion.1, bf16[4,4,1024,1024]{3,2,1,0:T(8,128)(2,1)} %param.4, s32[1024,1024]{1,0:T(8,128)} %broadcast_xor_fusion, s32[4,4]{1,0:T(4,128)S(1)} %broadcast_xor_fusion.3), kind=kOutput, calls=%fused_computation.9 | convolution fusion | flops 68753031168 | bytes 88080448 | tf_op jit(solution)/shard_map/dot_general | solution.py:20
  315.2 0.0 reduce-scatter.2.cloned.1.call-update
  315.2 0.0 all-reduce.2.cloned.1.call-start
  315.3 205.6 %reduce-scatter.2.cloned.1.call-done = f32[4,1024,2,128]{3,1,2,0:T(8,128)} async-done(((f32[4,1024,2,1024]{3,1,2,0:T(8,128)}), f32[4,1024,2,128]{3,1,2,0:T(8,128)}) %reduce-scatter.2.cloned.1.call-update) | async-done | bytes 4194320 | tf_op jit(solution)/shard_map/reduce_scatter | solution.py:51
  520.8 0.0 all-reduce.2.cloned.1.call-update
  520.9 157.5 %all-reduce.2.cloned.1.call-done = f32[4,1024,2,128]{3,1,2,0:T(8,128)} async-done(((f32[4,1024,2,128]{3,1,2,0:T(8,128)}), f32[4,1024,2,128]{3,1,2,0:T(8,128)}) %all-reduce.2.cloned.1.call-update) | async-done | bytes 4194320 | tf_op jit(solution)/shard_map/psum | solution.py:52
  678.3 7.4 %copy.11 = f32[4,1024,2,128]{3,2,1,0:T(2,128)} copy(f32[4,1024,2,128]{3,1,2,0:T(8,128)} %all-reduce.2.cloned.1.call-done) | data formatting | bytes 8388608 | tf_op jit(solution)/shard_map/psum | solution.py:52
Async XLA Ops:
  28.6 5.9 copy-start.1
  28.6 6.1 copy-start
  28.6 190.5 %all-to-all-start = ((bf16[32,128,2,1024]{3,1,2,0:T(8,128)(2,1)}), bf16[32,128,2,1024]{3,1,2,0:T(8,128)(2,1)}, u32[]{:S(2)}, u32[]{:S(2)}) async-start(bf16[32,128,2,1024]{3,1,2,0:T(8,128)(2,1)} %bitcast.27), calls=%async_computation | async-start | bytes 33554432 | tf_op jit(solution)/shard_map/all_to_all | solution.py:40
  34.5 486.3 %reduce-scatter.2.cloned.1.call-start = ((), (), s32[]{:S(2)}) async-start(), calls=%async_computation.2 | async-start | bytes 37748736 | tf_op jit(solution)/shard_map/reduce_scatter | solution.py:51
  315.2 363.1 %all-reduce.2.cloned.1.call-start = ((), (), s32[]{:S(2)}) async-start(), calls=%async_computation.3 | async-start | bytes 8388608 | tf_op jit(solution)/shard_map/psum | solution.py:52
Sparse Core Ops, SparseCore 0:
  315.3 205.4 reduce-scatter.1
  523.3 154.9 all-reduce.1
where the time goes:
time: 693 us
  waiting for transfers between devices  545 us (79%)
  matrix products  79 us (11%)
  local copies, waits for them, and re-layouts  38.1 us (5%)
  between operations  13.5 us (2%)
  other arithmetic  11.2 us (2%)
    reduce_scatter x1, waiting for transfers between devices, body(): lax.psum_scatter(partial_value, 'redist', scatter_dimension=3, tiled=True)  206 us
    all_to_all x1, waiting for transfers between devices, body(): lax.all_to_all(ints_mine, 'redist', split_axis=0, concat_axis=1, tiled=True)  182 us
    psum x1, waiting for transfers between devices, body(): return lax.psum(shares, 'rep')  157 us
    dot_general x1, matrix products, contract(): lax.dot_general(masked, operand, (((1, 3), (0, 1)), ((), ())), preferred_...  79 us
  transfers between devices with their start and end apart: 3, of which 3 were waited for; matrix products, arithmetic and copies ran while one was open for 0% of the time, Pallas kernels for 0%

commit v1 on v0

v1 whole, which is shorter than its diff:
```python
import jax
import jax.numpy as jnp
from jax import lax
from jax.sharding import PartitionSpec as P


def fold(array, axis, width):
    size = array.shape[axis]
    total = None
    for start in range(0, size, width):
        piece = lax.slice_in_dim(array, start, min(start + width, size), axis=axis)
        short = width - piece.shape[axis]
        if short:
            pads = [(0, 0, 0)] * array.ndim
            pads[axis] = (0, short, 0)
            piece = lax.pad(piece, jnp.zeros((), array.dtype), pads)
        total = piece if total is None else total + piece
    return total


def unfold(array, axis, size):
    width = array.shape[axis]
    copies = -(-size // width)
    return lax.slice_in_dim(jnp.concatenate([array] * copies, axis=axis), 0, size, axis=axis)


def body(amplitudes, integrals, occ_irrep, virt_irrep):
    n_redist = lax.axis_size("redist")
    n_rep = lax.axis_size("rep")
    dev_index = lax.axis_index("redist")
    rep_index = lax.axis_index("rep")
    i_slab, k_block, virt, _ = amplitudes.shape
    c_block = integrals.shape[1]
    j_slab = integrals.shape[2]
    b_block = virt // n_redist
    width = 3 * virt // 16
    zero = jnp.zeros((), amplitudes.dtype)
    slab_label = occ_irrep[0]

    grouped = integrals.reshape(n_redist, n_rep, k_block, c_block, j_slab, virt)
    mine = lax.dynamic_slice_in_dim(grouped, rep_index, 1, 1)[:, 0]
    k_labels = lax.dynamic_slice_in_dim(
        occ_irrep.reshape(n_redist, n_rep, k_block), rep_index, 1, 1
    )[:, 0]
    c_labels = lax.dynamic_slice_in_dim(virt_irrep, dev_index * c_block, c_block)
    want = k_labels[:, :, None] ^ c_labels[None, None, :] ^ slab_label
    keep = want[:, :, :, None, None] == virt_irrep
    folded = fold(jnp.where(keep, mine, zero), 4, width)
    folded = folded.reshape(n_redist * k_block, c_block, j_slab * width)
    moved = lax.all_to_all(folded, "redist", split_axis=0, concat_axis=1, tiled=True)

    my_k = lax.dynamic_slice_in_dim(occ_irrep, (dev_index * n_rep + rep_index) * k_block, k_block)
    pair = my_k[:, None] ^ virt_irrep[None, :] ^ slab_label
    masked = jnp.where(pair[:, None, :] == virt_irrep[None, :, None], amplitudes, zero)
    amps = fold(masked, 2, width)

    wide = unfold(moved.reshape(k_block, virt, j_slab, width), 3, virt)
    sym = jnp.where(pair[:, :, None, None] == virt_irrep, wide, zero)
    part = lax.dot_general(
        amps, sym, (((1, 3), (0, 1)), ((), ())), preferred_element_type=jnp.float32
    )
    share = lax.psum_scatter(part, "redist", scatter_dimension=3, tiled=True)
    share = lax.psum(share, "rep")

    b_labels = lax.dynamic_slice_in_dim(virt_irrep, dev_index * b_block, b_block)
    out_keep = virt_irrep[:, None, None] == b_labels
    return jnp.where(out_keep, unfold(share, 1, virt), jnp.zeros((), jnp.float32))


def solution(mesh):
    placed = (P(None, ("redist", "rep"), None, None), P(None, "redist", None, None), P(), P())
    return jax.shard_map(
        body, mesh=mesh, in_specs=placed, out_specs=P(None, None, None, "redist"), check_vma=False
    )
```

time: 693 us -> 297 us (0.43)
  waiting for transfers between devices: 545 us -> 112 us
  matrix products: 79 us -> 24.6 us
  local copies, waits for them, and re-layouts: 38.1 us -> 88.2 us
  other arithmetic: 11.2 us -> 52.3 us
    all_to_all x1, waiting for transfers between devices: 182 us -> 4.66 us  [body(): lax.all_to_all(folded, 'redist', split_axis=0, concat_axis=1, tiled=True)]
    reduce_scatter x1, waiting for transfers between devices: 206 us -> 61 us  [body(): share = lax.psum_scatter(part, 'redist', scatter_dimension=3, tiled=True)]
    psum x1, waiting for transfers between devices: 157 us -> 45.9 us  [body(): share = lax.psum(share, 'rep')]
    dot_general x1, matrix products: 79 us -> 24.6 us  [body(): lax.dot_general(amps, sym, (((1, 3), (0, 1)), ((), ())), preferred_elemen...]
    unnamed x5 -> x17, local copies, waits for them, and re-layouts: 8.77 us -> 57 us
    select_n x1 -> x3, other arithmetic: 8.59 us -> 33.5 us  [the longest x1 24.4 us: body(): jnp.where(pair[:, None, :] == virt_irrep[None, :, None], amplitudes, zero)]
    eq x0 -> x4, other arithmetic: none -> 13.9 us  [the longest x1 5.13 us: body(): keep = want[:, :, :, None, None] == virt_irrep]
    psum x1 -> x0, local copies, waits for them, and re-layouts: 7.43 us -> none  [body(): return lax.psum(shares, 'rep')]
  transfers between devices with their start and end apart: 3 -> 3, of which waited for: 3 -> 3; matrix products, arithmetic and copies ran while one was open for 0% -> 11% of each run, Pallas kernels for 0% -> 0%
where the time goes in v1:
time: 297 us; the launch traced here: 296 us
  waiting for transfers between devices  112 us (38%)
  local copies, waits for them, and re-layouts  88.2 us (30%)
  other arithmetic  52.3 us (18%)
  matrix products  24.6 us (8%)
  between operations  13.5 us (5%)
  starting transfers between devices  5.6 us (2%)
    reduce_scatter x1, waiting for transfers between devices, body(): share = lax.psum_scatter(part, 'redist', scatter_dimension=3, tiled=True)  61 us
    unnamed x17, local copies, waits for them, and re-layouts  57 us
    psum x1, waiting for transfers between devices, body(): share = lax.psum(share, 'rep')  45.9 us
    dot_general x1, matrix products, body(): lax.dot_general(amps, sym, (((1, 3), (0, 1)), ((), ())), preferred_elemen...  24.6 us
    select_n x1, other arithmetic, body(): jnp.where(pair[:, None, :] == virt_irrep[None, :, None], amplitudes, zero)  24.4 us
    dynamic_slice x1, local copies, waits for them, and re-layouts, body(): mine = lax.dynamic_slice_in_dim(grouped, rep_index, 1, 1)[:, 0]  14.3 us
    select_n x1, other arithmetic, body(): folded = fold(jnp.where(keep, mine, zero), 4, width)  8.86 us
  transfers between devices with their start and end apart: 3, of which 3 were waited for; matrix products, arithmetic and copies ran while one was open for 11% of the time, Pallas kernels for 0%

profile of v1, /device:TPU:0, one launch (start us, length us, event | category | flops | bytes accessed | tf_op | source)
XLA Modules:
  0.0 295.9 jit_solution(6883255731468440052)
XLA Ops:
  6.5 0.8 reshape.100
  7.3 0.8 dynamic_slice.13
  8.1 0.7 xor_xor_fusion
  8.8 5.1 %broadcast_compare_fusion = pred[8,4,128,1024]{2,3,1,0:T(8,128)(4,1)} fusion(s32[8,4,128]{2,1,0:T(4,128)S(1)} %xor_xor_fusion, s32[1024]{0:T(1024)} %param.7), kind=kLoop, calls=%fused_computation.7 | loop fusion | flops 4194304 | bytes 4214784 | tf_op jit(solution)/shard_map/eq | solution.py:47
  13.9 14.3 %constant_dynamic-slice_fusion = bf16[8,1,4,128,2,1024]{5,4,3,2,1,0:T(2,128)(2,1)} fusion(bf16[8,4,4,128,2,1024]{5,4,3,2,1,0:T(2,128)(2,1)} %bitcast.4, s32[]{:T(128)S(6)} %select_n.30), kind=kLoop, calls=%fused_computation.41 | loop fusion | bytes 33554436 | tf_op jit(solution)/shard_map/dynamic_slice | solution.py:41
  28.2 41.0 %copy.20 = bf16[8,1,4,128,2,1024]{3,5,4,2,0,1:T(8,128)(2,1)} copy(bf16[8,1,4,128,2,1024]{5,4,3,2,1,0:T(2,128)(2,1)} %constant_dynamic-slice_fusion) | data formatting | bytes 33554432
  69.2 8.9 %bitcast_select_fusion = bf16[8,4,128,2,1024]{2,4,3,1,0:T(8,128)(2,1)S(1)} fusion(bf16[8,1,4,128,2,1024]{3,5,4,2,0,1:T(8,128)(2,1)} %copy.20, pred[8,4,128,1024]{2,3,1,0:T(8,128)(4,1)} %broadcast_compare_fusion), kind=kLoop, calls=%fused_computation.4 | loop fusion | flops 8388608 | bytes 37748736 | tf_op jit(solution)/shard_map/jit(_where)/select_n | solution.py:48
  78.1 4.0 %fusion.10 = bf16[8,4,128,2,192]{2,4,3,1,0:T(8,128)(2,1)} fusion(bf16[8,4,128,2,1024]{2,4,3,1,0:T(8,128)(2,1)S(1)} %bitcast_select_fusion, bf16[8,4,128,2,64]{2,4,3,1,0:T(8,128)(2,1)S(1)} %slice.71), kind=kLoop, calls=%fused_computation.20 | loop fusion | flops 18874368 | bytes 19922944 | tf_op jit(solution)/shard_map/add | solution.py:17
  82.2 5.3 %all-to-all-start = ((bf16[32,128,384]{1,2,0:T(8,128)(2,1)}), bf16[32,128,384]{1,2,0:T(8,128)(2,1)S(1)}, u32[]{:S(2)}, u32[]{:S(2)}) async-start(bf16[32,128,384]{1,2,0:T(8,128)(2,1)} %bitcast.6), calls=%async_computation | async-start | bytes 6291456 | tf_op jit(solution)/shard_map/all_to_all | solution.py:50
  87.7 4.3 %broadcast_compare_fusion.2 = pred[4,1024,1024]{2,1,0:T(8,128)(4,1)} fusion(s32[4,1024]{1,0:T(4,128)S(1)} %xor_xor_fusion.1, s32[1024]{0:T(1024)S(1)} %copy-done.1), kind=kLoop, calls=%fused_computation.9 | loop fusion | flops 4194304 | bytes 4214784 | tf_op jit(solution)/shard_map/eq | solution.py:54
  92.0 24.4 %broadcast_select_fusion = bf16[4,4,1024,1024]{3,2,1,0:T(8,128)(2,1)} fusion(bf16[4,4,1024,1024]{3,2,1,0:T(8,128)(2,1)} %param.4, pred[4,1024,1024]{2,1,0:T(8,128)(4,1)} %broadcast_compare_fusion.2), kind=kLoop, calls=%fused_computation | loop fusion | flops 16777216 | bytes 71303168 | tf_op jit(solution)/shard_map/jit(_where)/select_n | solution.py:54
  116.4 4.3 %broadcast_compare_fusion.1 = pred[4,1024,1024]{1,2,0:T(8,128)(4,1)} fusion(s32[4,1024]{1,0:T(4,128)S(1)} %xor_xor_fusion.1, s32[1024]{0:T(1024)S(1)} %copy-done.1), kind=kLoop, calls=%fused_computation.8 | loop fusion | flops 4194304 | bytes 4214784 | tf_op jit(solution)/shard_map/eq | solution.py:58
  120.7 4.7 %all-to-all-done = bf16[32,128,384]{1,2,0:T(8,128)(2,1)S(1)} async-done(((bf16[32,128,384]{1,2,0:T(8,128)(2,1)}), bf16[32,128,384]{1,2,0:T(8,128)(2,1)S(1)}, u32[]{:S(2)}, u32[]{:S(2)}) %all-to-all-start) | async-done | bytes 3145760 | tf_op jit(solution)/shard_map/all_to_all | solution.py:50
  125.4 3.6 %copy.22 = bf16[8,4,128,384]{2,0,3,1:T(8,128)(2,1)} copy(bf16[8,4,128,384]{2,3,1,0:T(8,128)(2,1)S(1)} %bitcast.34) | data formatting | bytes 6291456 | tf_op jit(solution)/shard_map/all_to_all | solution.py:50
  129.0 4.1 %reshape.103 = bf16[4,1024,2,192]{1,3,2,0:T(8,128)(2,1)S(1)} reshape(bf16[4,8,128,384]{2,1,3,0:T(8,128)(2,1)} %bitcast.35) | data formatting | bytes 6291456 | tf_op jit(solution)/shard_map/reshape | solution.py:57
  133.1 2.3 constant_dynamic-update-slice_fusion.5
  135.4 2.2 constant_dynamic-update-slice_fusion.4
  137.6 2.2 constant_dynamic-update-slice_fusion.3
  139.8 2.2 constant_dynamic-update-slice_fusion.2
  142.1 2.2 constant_dynamic-update-slice_fusion.1
  144.3 2.1 constant_dynamic-update-slice_fusion
  146.4 24.6 %fusion.11 = f32[4,192,2,1024]{3,1,2,0:T(8,128)} fusion(bf16[4,1024,2,1152]{1,3,2,0:T(8,128)(2,1)} %constant_dynamic-update-slice_fusion, pred[4,1024,1024]{1,2,0:T(8,128)(4,1)} %broadcast_compare_fusion.1, bf16[4,4,1024,1024]{3,2,1,0:T(8,128)(2,1)} %broadcast_select_fusion, bf16[4,4,64,1024]{3,2,1,0:T(8,128)(2,1)S(1)} %slice-done), kind=kOutput, calls=%fused_computation.25 | convolution fusion | flops 12931039232 | bytes 60817408 | tf_op jit(solution)/shard_map/dot_general | solution.py:59
  171.0 0.3 all-reduce.4.cloned.1.call-start
  171.3 61.0 %reduce-scatter.2.cloned.1.call-done = f32[4,192,2,128]{3,1,2,0:T(8,128)} async-done(((f32[4,192,2,1024]{3,1,2,0:T(8,128)}), f32[4,192,2,128]{3,1,2,0:T(8,128)}) %reduce-scatter.2.cloned.1.call-update) | async-done | bytes 786448 | tf_op jit(solution)/shard_map/reduce_scatter | solution.py:62
  232.3 0.2 broadcast_compare_fusion.3
  232.6 45.9 %all-reduce.4.cloned.1.call-done = f32[4,192,2,128]{3,1,2,0:T(8,128)} async-done(((f32[4,192,2,128]{3,1,2,0:T(8,128)}), f32[4,192,2,128]{3,1,2,0:T(8,128)}) %all-reduce.4.cloned.1.call-update) | async-done | bytes 786448 | tf_op jit(solution)/shard_map/psum | solution.py:63
  278.5 1.3 constant_dynamic-update-slice_fusion.11
  279.8 1.2 constant_dynamic-update-slice_fusion.10
  280.9 1.2 constant_dynamic-update-slice_fusion.9
  282.1 1.2 constant_dynamic-update-slice_fusion.8
  283.5 0.3 slice_select_fusion.1
  283.8 5.2 %copy.13 = f32[4,1024,2,128]{3,2,1,0:T(2,128)} copy(f32[4,1024,2,128]{3,1,2,0:T(8,128)S(1)} %slice_select_fusion.1) | data formatting | bytes 8388608 | tf_op jit(solution)/shard_map/jit(_where)/select_n | solution.py:67
  (17 shorter events, 0.5 us)
Async XLA Ops:
  82.2 5.4 %copy-start.2 = (s32[128]{0:T(128)S(1)}, s32[128]{0:T(128)}, u32[]{:S(2)}) copy-start(s32[128]{0:T(128)} %param.6) | copy-start | bytes 1540
  82.2 5.4 %copy-start.1 = (s32[1024]{0:T(1024)S(1)}, s32[1024]{0:T(1024)}, u32[]{:S(2)}) copy-start(s32[1024]{0:T(1024)} %param.7) | copy-start | bytes 12292
  82.2 43.2 %all-to-all-start = ((bf16[32,128,384]{1,2,0:T(8,128)(2,1)}), bf16[32,128,384]{1,2,0:T(8,128)(2,1)S(1)}, u32[]{:S(2)}, u32[]{:S(2)}) async-start(bf16[32,128,384]{1,2,0:T(8,128)(2,1)} %bitcast.6), calls=%async_computation | async-start | bytes 6291456 | tf_op jit(solution)/shard_map/all_to_all | solution.py:50
  87.5 144.8 %reduce-scatter.2.cloned.1.call-start = ((), (), s32[]{:S(2)}) async-start(), calls=%async_computation.2 | async-start | bytes 7077888 | tf_op jit(solution)/shard_map/reduce_scatter | solution.py:62
  142.0 4.4 %slice-start = ((bf16[4,4,1024,1024]{3,2,1,0:T(8,128)(2,1)}), bf16[4,4,64,1024]{3,2,1,0:T(8,128)(2,1)S(1)}, s32[]{:S(2)}) async-start(bf16[4,4,1024,1024]{3,2,1,0:T(8,128)(2,1)} %broadcast_select_fusion), calls=%async_computation.4 | async-start | bytes 4194304 | tf_op jit(solution)/shard_map/slice | solution.py:11
  171.0 107.5 %all-reduce.4.cloned.1.call-start = ((), (), s32[]{:S(2)}) async-start(), calls=%async_computation.3 | async-start | bytes 1572864 | tf_op jit(solution)/shard_map/psum | solution.py:63
  278.5 4.8 %copy-start = (f32[4,192,2,128]{3,1,2,0:T(8,128)S(1)}, f32[4,192,2,128]{3,1,2,0:T(8,128)}, u32[]{:S(2)}) copy-start(f32[4,192,2,128]{3,1,2,0:T(8,128)} %all-reduce.4.cloned.1.call-done) | copy-start | bytes 2359300
Sparse Core Ops, SparseCore 0:
  171.2 61.1 reduce-scatter.1
  234.8 43.6 all-reduce.3

commit v2 on v1

--- a/solution.py
+++ b/solution.py
@@ -1,7 +1,13 @@
+import functools
+
 import jax
 import jax.numpy as jnp
 from jax import lax
+from jax.experimental import pallas as pl
+from jax.experimental.pallas import tpu as pltpu
 from jax.sharding import PartitionSpec as P
+
+LANES = 128
 
 
 def fold(array, axis, width):
@@ -24,6 +30,108 @@
     return lax.slice_in_dim(jnp.concatenate([array] * copies, axis=axis), 0, size, axis=axis)
 
 
+def spans(j_slab, width):
+    found = []
+    for j in range(j_slab):
+        low = j * width // LANES * LANES
+        high = -(-(j + 1) * width // LANES) * LANES
+        found.append((low, high, j * width - low))
+    return found
+
+
+def one_hot(virt, width, low, high, shift):
+    place = jnp.arange(virt, dtype=jnp.int32) % width + shift
+    return (place[:, None] == jnp.arange(high - low, dtype=jnp.int32)).astype(jnp.bfloat16)
+
+
+def fold_kernel(cuts, _, want_ref, labels_ref, ints_ref, *rest):
+    hots, out_ref = rest[:-1], rest[-1]
+    keep = jnp.where(want_ref[0] == labels_ref[...], 1.0, 0.0).astype(jnp.bfloat16)
+    tiles = [None] * (out_ref.shape[-1] // LANES)
+    for j, (low, high, _) in enumerate(cuts):
+        sums = jnp.dot(
+            ints_ref[0, :, j, :] * keep, hots[j][...], preferred_element_type=jnp.float32
+        )
+        for tile in range(low // LANES, high // LANES):
+            piece = sums[:, tile * LANES - low : (tile + 1) * LANES - low]
+            tiles[tile] = piece if tiles[tile] is None else tiles[tile] + piece
+    for tile, value in enumerate(tiles):
+        out_ref[0, :, tile * LANES : (tile + 1) * LANES] = value.astype(jnp.bfloat16)
+
+
+def fold_integrals(integrals, want, virt_irrep, rep_index, n_redist, n_rep, k_block, width):
+    c_block, j_slab, virt = integrals.shape[1:]
+    cuts = spans(j_slab, width)
+    hots = [one_hot(virt, width, *cut) for cut in cuts]
+    packed = cuts[-1][1]
+
+    def source(d, k, rep):
+        return ((d * n_rep + rep[0]) * k_block + k, 0, 0, 0)
+
+    return pl.pallas_call(
+        functools.partial(fold_kernel, cuts),
+        out_shape=jax.ShapeDtypeStruct((n_redist * k_block, c_block, packed), jnp.bfloat16),
+        grid_spec=pltpu.PrefetchScalarGridSpec(
+            num_scalar_prefetch=1,
+            grid=(n_redist, k_block),
+            in_specs=[
+                pl.BlockSpec((1, c_block, 1), lambda d, k, rep: (d * k_block + k, 0, 0)),
+                pl.BlockSpec((1, virt), lambda d, k, rep: (0, 0)),
+                pl.BlockSpec((1, c_block, j_slab, virt), source),
+            ]
+            + [pl.BlockSpec(hot.shape, lambda d, k, rep: (0, 0)) for hot in hots],
+            out_specs=pl.BlockSpec((1, c_block, packed), lambda d, k, rep: (d * k_block + k, 0, 0)),
+        ),
+        compiler_params=pltpu.CompilerParams(vmem_limit_bytes=32 << 20),
+        name="fold_integrals",
+    )(rep_index[None], want, virt_irrep[None, :], integrals, *hots)
+
+
+def contract_kernel(low, high, want_ref, labels_ref, amps_ref, ints_ref, hot_ref, out_ref):
+    wide = jnp.dot(
+        ints_ref[0, :, low:high], hot_ref[...], preferred_element_type=jnp.float32
+    )
+    sym = jnp.where(want_ref[0] == labels_ref[...], wide, 0.0).astype(jnp.bfloat16)
+    k = pl.program_id(1)
+    for i in range(amps_ref.shape[0]):
+        part = jnp.dot(amps_ref[i, 0], sym, preferred_element_type=jnp.float32)
+
+        @pl.when(k == 0)
+        def _():
+            out_ref[i] = part
+
+        @pl.when(k > 0)
+        def _():
+            out_ref[i] += part
+
+
+def contract(amps, moved, want, virt_irrep, cut, width):
+    i_slab, k_block, _, virt = amps.shape
+    low, high, shift = cut
+    hot = one_hot(virt, width, low, high, shift).T
+    step = min(virt, 512)
+    return pl.pallas_call(
+        functools.partial(contract_kernel, low, high),
+        out_shape=jax.ShapeDtypeStruct((i_slab, width, virt), jnp.float32),
+        grid=(virt // step, k_block),
+        in_specs=[
+            pl.BlockSpec((1, virt, 1), lambda n, k: (k, 0, 0)),
+            pl.BlockSpec((1, step), lambda n, k: (0, n)),
+            pl.BlockSpec((i_slab, 1, width, virt), lambda n, k: (0, k, 0, 0)),
+            pl.BlockSpec((1, virt, moved.shape[2]), lambda n, k: (k, 0, 0)),
+            pl.BlockSpec((high - low, step), lambda n, k: (0, n)),
+        ],
+        out_specs=pl.BlockSpec((i_slab, width, step), lambda n, k: (0, 0, n)),
+        compiler_params=pltpu.CompilerParams(vmem_limit_bytes=48 << 20),
+        cost_estimate=pl.CostEstimate(
+            flops=2 * i_slab * k_block * width * virt * virt,
+            bytes_accessed=2 * (amps.size * 2 + moved.size * 2) + 4 * i_slab * width * virt,
+            transcendentals=0,
+        ),
+        name="contract",
+    )(want, virt_irrep[None, :], amps, moved, hot)
+
+
 def body(amplitudes, integrals, occ_irrep, virt_irrep):
     n_redist = lax.axis_size("redist")
     n_rep = lax.axis_size("rep")
@@ -37,16 +145,14 @@
     zero = jnp.zeros((), amplitudes.dtype)
     slab_label = occ_irrep[0]
 
-    grouped = integrals.reshape(n_redist, n_rep, k_block, c_block, j_slab, virt)
-    mine = lax.dynamic_slice_in_dim(grouped, rep_index, 1, 1)[:, 0]
     k_labels = lax.dynamic_slice_in_dim(
         occ_irrep.reshape(n_redist, n_rep, k_block), rep_index, 1, 1
-    )[:, 0]
+    ).reshape(n_redist * k_block)
     c_labels = lax.dynamic_slice_in_dim(virt_irrep, dev_index * c_block, c_block)
-    want = k_labels[:, :, None] ^ c_labels[None, None, :] ^ slab_label
-    keep = want[:, :, :, None, None] == virt_irrep
-    folded = fold(jnp.where(keep, mine, zero), 4, width)
-    folded = folded.reshape(n_redist * k_block, c_block, j_slab * width)
+    want = k_labels[:, None] ^ c_labels[None, :] ^ slab_label
+    folded = fold_integrals(
+        integrals, want[:, :, None], virt_irrep, rep_index, n_redist, n_rep, k_block, width
+    )
     moved = lax.all_to_all(folded, "redist", split_axis=0, concat_axis=1, tiled=True)
 
     my_k = lax.dynamic_slice_in_dim(occ_irrep, (dev_index * n_rep + rep_index) * k_block, k_block)
@@ -54,13 +160,12 @@
     masked = jnp.where(pair[:, None, :] == virt_irrep[None, :, None], amplitudes, zero)
     amps = fold(masked, 2, width)
 
-    wide = unfold(moved.reshape(k_block, virt, j_slab, width), 3, virt)
-    sym = jnp.where(pair[:, :, None, None] == virt_irrep, wide, zero)
-    part = lax.dot_general(
-        amps, sym, (((1, 3), (0, 1)), ((), ())), preferred_element_type=jnp.float32
-    )
-    share = lax.psum_scatter(part, "redist", scatter_dimension=3, tiled=True)
-    share = lax.psum(share, "rep")
+    shares = []
+    for cut in spans(j_slab, width):
+        part = contract(amps, moved, pair[:, :, None], virt_irrep, cut, width)
+        share = lax.psum_scatter(part, "redist", scatter_dimension=2, tiled=True)
+        shares.append(lax.psum(share, "rep"))
+    share = jnp.stack(shares, axis=2)
 
     b_labels = lax.dynamic_slice_in_dim(virt_irrep, dev_index * b_block, b_block)
     out_keep = virt_irrep[:, None, None] == b_labels

time: 297 us -> 290 us (0.976)
  Pallas kernels: 0 us -> 82 us
  local copies, waits for them, and re-layouts: 88.2 us -> 12.9 us
  matrix products: 24.6 us -> 0 us
  waiting for transfers between devices: 112 us -> 126 us
    pallas_call x0 -> x3, Pallas kernels: none -> 82 us  [the longest x1 44.2 us: fold_integrals(): pl.pallas_call(functools.partial(fold_kernel, cuts), out_shape=jax.ShapeD...]
    unnamed x17 -> x10, local copies, waits for them, and re-layouts: 57 us -> 0.7 us
    dot_general x1 -> x0, matrix products: 24.6 us -> none  [body(): lax.dot_general(amps, sym, (((1, 3), (0, 1)), ((), ())), preferred_elemen...]
    reduce_scatter x1 -> x2, waiting for transfers between devices: 61 us -> 79.4 us  [body(): share = lax.psum_scatter(part, 'redist', scatter_dimension=2, tiled=True)]
    dynamic_slice x1 -> x0, local copies, waits for them, and re-layouts: 14.3 us -> none  [body(): mine = lax.dynamic_slice_in_dim(grouped, rep_index, 1, 1)[:, 0]]
    add x1, other arithmetic: 4.04 us -> 15.2 us  [fold(): total = piece if total is None else total + piece]
    eq x2 -> x0, other arithmetic: 9.44 us -> none  [the longest x1 5.13 us: body(): keep = want[:, :, :, None, None] == virt_irrep]
    select_n x1, other arithmetic: 8.86 us -> 0.01 us  [one_hot(): place = jnp.arange(virt, dtype=jnp.int32) % width + shift]
  transfers between devices with their start and end apart: 3 -> 4, of which waited for: 3 -> 3; matrix products, arithmetic and copies ran while one was open for 11% -> 15% of each run, Pallas kernels for 0% -> 7%
where the time goes in v2:
time: 290 us; the launch traced here: 289 us
  waiting for transfers between devices  126 us (43%)
  Pallas kernels  82 us (28%)
  other arithmetic  49.9 us (17%)
  between operations  13.3 us (5%)
  local copies, waits for them, and re-layouts  12.9 us (4%)
  starting transfers between devices  5.6 us (2%)
    reduce_scatter x2, waiting for transfers between devices, body(): share = lax.psum_scatter(part, 'redist', scatter_dimension=2, tiled=True)  79.4 us
    psum x1, waiting for transfers between devices, body(): shares.append(lax.psum(share, 'rep'))  46.3 us
    pallas_call x1, Pallas kernels, fold_integrals(): pl.pallas_call(functools.partial(fold_kernel, cuts), out_shape=jax.ShapeD...  44.2 us
    pallas_call x2, Pallas kernels, contract(): pl.pallas_call(functools.partial(contract_kernel, low, high), out_shape=j...  37.7 us
    select_n x1, other arithmetic, body(): jnp.where(pair[:, None, :] == virt_irrep[None, :, None], amplitudes, zero)  24.2 us
    add x1, other arithmetic, fold(): total = piece if total is None else total + piece  15.2 us
  transfers between devices with their start and end apart: 4, of which 3 were waited for; matrix products, arithmetic and copies ran while one was open for 15% of the time, Pallas kernels for 7%

profile of v2, /device:TPU:0, one launch (start us, length us, event | category | flops | bytes accessed | tf_op | source)
XLA Modules:
  0.0 289.4 jit_solution(6363487245026681545)
XLA Ops:
  6.6 0.8 reshape.151
  7.4 0.1 xor.96
  7.4 0.8 dynamic_slice.10
  8.2 0.3 fusion.1
  8.5 1.0 xor_xor_fusion.want_ref
  9.6 0.7 copy-done
  10.2 44.2 %fold_integrals.1 = bf16[32,128,384]{2,1,0:T(8,128)(2,1)} custom-call(s32[1]{0:T(128)} %bitcast.2._, s32[32,128,1]{2,1,0:T(8,128)S(1)} %xor_xor_fusion.want_ref, s32[1,1024]{1,0:T(1,128)S(1)} %bitcast.10, bf16[128,128,2,1024]{3,2,1,0:T(2,128)(2,1)} %ints_ref.1, bf16[1024,256]{1,0:T(8,128)(2,1)S(1)} %get-tuple-element.7.rest_0_, ...), custom_call_target="tpu_custom_call" | custom-call | tf_op jit(solution)/shard_map/fold_integrals/pallas_call | solution.py:71
  54.5 5.3 %all-to-all-start = ((bf16[32,128,384]{2,1,0:T(8,128)(2,1)}), bf16[32,128,384]{2,1,0:T(8,128)(2,1)}, u32[]{:S(2)}, u32[]{:S(2)}) async-start(bf16[32,128,384]{2,1,0:T(8,128)(2,1)} %fold_integrals.1), calls=%async_computation | async-start | bytes 6291456 | tf_op jit(solution)/shard_map/all_to_all | solution.py:156
  59.8 0.1 dynamic_slice.11
  59.9 0.1 xor_xor_fusion.2
  60.0 4.3 %broadcast_compare_fusion = pred[4,1024,1024]{2,1,0:T(8,128)(4,1)} fusion(s32[4,1024]{1,0:T(4,128)S(1)} %xor_xor_fusion.2, s32[1024]{0:T(1024)S(1)} %copy-done.1), kind=kLoop, calls=%fused_computation.1 | loop fusion | flops 4194304 | bytes 4214784 | tf_op jit(solution)/shard_map/eq | solution.py:160
  64.3 24.2 %broadcast_select_fusion = bf16[4,4,1024,1024]{3,2,1,0:T(8,128)(2,1)} fusion(bf16[4,4,1024,1024]{3,2,1,0:T(8,128)(2,1)} %param.4, pred[4,1024,1024]{2,1,0:T(8,128)(4,1)} %broadcast_compare_fusion), kind=kLoop, calls=%fused_computation | loop fusion | flops 16777216 | bytes 71303168 | tf_op jit(solution)/shard_map/jit(_where)/select_n | solution.py:160
  88.5 0.1 fusion.3.hot_ref
  88.6 0.3 xor_xor_fusion.1.want_ref
  88.9 1.2 slice-done
  90.1 15.2 %fusion.amps_ref = bf16[4,4,192,1024]{3,2,1,0:T(8,128)(2,1)} fusion(bf16[4,4,1024,1024]{3,2,1,0:T(8,128)(2,1)} %broadcast_select_fusion, bf16[4,4,64,1024]{3,2,1,0:T(8,128)(2,1)S(1)} %slice-done), kind=kLoop, calls=%fused_computation.3 | loop fusion | flops 37748736 | bytes 39845888 | tf_op jit(solution)/shard_map/add | solution.py:23
  105.3 4.1 %copy.10 = bf16[8,4,128,384]{3,2,0,1:T(8,128)(2,1)} copy(bf16[8,4,128,384]{3,2,1,0:T(8,128)(2,1)} %bitcast.3) | data formatting | bytes 6291456 | tf_op jit(solution)/shard_map/all_to_all | solution.py:156
  109.4 18.8 %contract.2 = f32[4,192,1024]{2,1,0:T(8,128)} custom-call(s32[4,1024,1]{2,1,0:T(8,128)S(1)} %xor_xor_fusion.1.want_ref, s32[1,1024]{1,0:T(1,128)S(1)} %bitcast.11, bf16[4,4,192,1024]{3,2,1,0:T(8,128)(2,1)} %fusion.amps_ref, bf16[4,1024,384]{2,1,0:T(8,128)(2,1)} %bitcast.13, bf16[256,1024]{1,0:T(8,128)(2,1)S(1)} %fusion.3.hot_ref), custom_call_target="tpu_custom_call" | custom-call | flops 6442450944 | bytes 22020096 | tf_op jit(solution)/shard_map/contract/pallas_call | solution.py:113
  128.2 0.1 fusion.4.hot_ref
  128.3 19.0 %contract.3 = f32[4,192,1024]{2,1,0:T(8,128)} custom-call(s32[4,1024,1]{2,1,0:T(8,128)S(1)} %xor_xor_fusion.1.want_ref, s32[1,1024]{1,0:T(1,128)S(1)} %bitcast.12, bf16[4,4,192,1024]{3,2,1,0:T(8,128)(2,1)} %fusion.amps_ref, bf16[4,1024,384]{2,1,0:T(8,128)(2,1)} %bitcast.14, bf16[256,1024]{1,0:T(8,128)(2,1)S(1)} %fusion.4.hot_ref), custom_call_target="tpu_custom_call" | custom-call | flops 6442450944 | bytes 22020096 | tf_op jit(solution)/shard_map/contract/pallas_call | solution.py:113
  147.3 0.2 all-reduce.4.cloned.1.call-start
  147.6 29.4 %reduce-scatter.3.cloned.1.call-done = f32[4,192,128]{2,1,0:T(8,128)} async-done(((f32[4,192,1024]{2,1,0:T(8,128)}), f32[4,192,128]{2,1,0:T(8,128)}) %reduce-scatter.3.cloned.1.call-update) | async-done | bytes 393232 | tf_op jit(solution)/shard_map/reduce_scatter | solution.py:166
  177.0 50.0 %reduce-scatter.5.cloned.1.call-done = f32[4,192,128]{2,1,0:T(8,128)} async-done(((f32[4,192,1024]{2,1,0:T(8,128)}), f32[4,192,128]{2,1,0:T(8,128)}) %reduce-scatter.5.cloned.1.call-update) | async-done | bytes 393232 | tf_op jit(solution)/shard_map/reduce_scatter | solution.py:166
  227.0 0.2 broadcast_compare_fusion.1
  227.2 46.3 %all-reduce.4.cloned.1.call-done = (f32[4,192,1,128]{3,1,0,2:T(8,128)}, f32[4,192,1,128]{3,1,0,2:T(8,128)}) async-done(((f32[4,192,1,128]{3,1,0,2:T(8,128)}, f32[4,192,1,128]{3,1,0,2:T(8,128)}), (f32[4,192,1,128]{3,1,0,2:T(8,128)}, f32[4,192,1,128]{3,1,0,2:T(8,128)})) %all-reduce.4.cloned.1.call-update) | async-done | bytes 786448 | tf_op jit(solution)/shard_map/psum | solution.py:167
  273.5 1.2 fusion.10
  274.7 1.2 fusion.9
  275.9 1.2 fusion.8
  277.1 0.1 fusion.7
  277.1 0.1 fusion.6
  277.3 0.3 slice_select_fusion
  277.6 5.2 %copy.11 = f32[4,1024,2,128]{3,2,1,0:T(2,128)} copy(f32[4,1024,2,128]{3,1,0,2:T(8,128)S(1)} %slice_select_fusion) | data formatting | bytes 8388608 | tf_op jit(solution)/shard_map/jit(_where)/select_n | solution.py:172
  (20 shorter events, 0.3 us)
Async XLA Ops:
  9.6 0.7 copy-start
  54.5 5.4 %copy-start.4 = (s32[128]{0:T(128)S(1)}, s32[128]{0:T(128)}, u32[]{:S(2)}) copy-start(s32[128]{0:T(128)} %param.6) | copy-start | bytes 1540
  54.5 5.4 %copy-start.1 = (s32[1024]{0:T(1024)S(1)}, s32[1024]{0:T(1024)}, u32[]{:S(2)}) copy-start(s32[1024]{0:T(1024)} %param.7) | copy-start | bytes 12292
  54.5 50.8 %all-to-all-start = ((bf16[32,128,384]{2,1,0:T(8,128)(2,1)}), bf16[32,128,384]{2,1,0:T(8,128)(2,1)}, u32[]{:S(2)}, u32[]{:S(2)}) async-start(bf16[32,128,384]{2,1,0:T(8,128)(2,1)} %fold_integrals.1), calls=%async_computation | async-start | bytes 6291456 | tf_op jit(solution)/shard_map/all_to_all | solution.py:156
  59.8 117.2 %reduce-scatter.3.cloned.1.call-start = ((), (), s32[]{:S(2)}) async-start(), calls=%async_computation.3 | async-start | bytes 3538944 | tf_op jit(solution)/shard_map/reduce_scatter | solution.py:166
  88.5 1.6 slice-start
  128.2 98.8 %reduce-scatter.5.cloned.1.call-start = ((), (), s32[]{:S(2)}) async-start(), calls=%async_computation.4 | async-start | bytes 3538944 | tf_op jit(solution)/shard_map/reduce_scatter | solution.py:166
  147.3 126.1 %all-reduce.4.cloned.1.call-start = ((), (), s32[]{:S(2)}) async-start(), calls=%async_computation.5 | async-start | bytes 1572864 | tf_op jit(solution)/shard_map/psum | solution.py:167
  273.5 3.6 %copy-start.2 = (f32[4,192,1,128]{3,1,0,2:T(8,128)S(1)}, f32[4,192,1,128]{3,1,0,2:T(8,128)}, u32[]{:S(2)}) copy-start(f32[4,192,1,128]{3,1,0,2:T(8,128)} %get-tuple-element.5) | copy-start | bytes 1179652
  273.5 3.6 %copy-start.3 = (f32[4,192,1,128]{3,1,0,2:T(8,128)S(1)}, f32[4,192,1,128]{3,1,0,2:T(8,128)}, u32[]{:S(2)}) copy-start(f32[4,192,1,128]{3,1,0,2:T(8,128)} %get-tuple-element.6) | copy-start | bytes 1179652
Sparse Core Ops, SparseCore 0:
  128.3 48.6 reduce-scatter.2
  180.7 46.1 reduce-scatter.4
  229.4 44.0 all-reduce.3

commit v3 on v2

v3 whole, which is shorter than its diff:
```python
import functools

import jax
import jax.numpy as jnp
from jax import lax
from jax.experimental import pallas as pl
from jax.experimental.pallas import tpu as pltpu
from jax.sharding import PartitionSpec as P

LANES = 128


def unfold(array, axis, size):
    width = array.shape[axis]
    copies = -(-size // width)
    return lax.slice_in_dim(jnp.concatenate([array] * copies, axis=axis), 0, size, axis=axis)


def spans(j_slab, width):
    found = []
    for j in range(j_slab):
        low = j * width // LANES * LANES
        high = -(-(j + 1) * width // LANES) * LANES
        found.append((low, high, j * width - low))
    return found


def one_hot(virt, width, low, high, shift):
    place = jnp.arange(virt, dtype=jnp.int32) % width + shift
    return (place[:, None] == jnp.arange(high - low, dtype=jnp.int32)).astype(jnp.bfloat16)


def fold_kernel(cuts, _, want_ref, labels_ref, ints_ref, *rest):
    hots, out_ref = rest[:-1], rest[-1]
    keep = jnp.where(want_ref[0] == labels_ref[...], 1.0, 0.0).astype(jnp.bfloat16)
    tiles = [None] * (out_ref.shape[-1] // LANES)
    for j, (low, high, _) in enumerate(cuts):
        sums = jnp.dot(
            ints_ref[0, :, j, :] * keep, hots[j][...], preferred_element_type=jnp.float32
        )
        for tile in range(low // LANES, high // LANES):
            piece = sums[:, tile * LANES - low : (tile + 1) * LANES - low]
            tiles[tile] = piece if tiles[tile] is None else tiles[tile] + piece
    for tile, value in enumerate(tiles):
        out_ref[0, :, tile * LANES : (tile + 1) * LANES] = value.astype(jnp.bfloat16)


def fold_integrals(integrals, want, virt_irrep, rep_index, sizes, first, count, width):
    n_redist, n_rep, k_block = sizes
    c_block, j_slab, virt = integrals.shape[1:]
    cuts = spans(j_slab, width)
    hots = [one_hot(virt, width, *cut) for cut in cuts]
    packed = cuts[-1][1]

    def source(d, k, rep):
        return ((d * n_rep + rep[0]) * k_block + first + k, 0, 0, 0)

    return pl.pallas_call(
        functools.partial(fold_kernel, cuts),
        out_shape=jax.ShapeDtypeStruct((n_redist * count, c_block, packed), jnp.bfloat16),
        grid_spec=pltpu.PrefetchScalarGridSpec(
            num_scalar_prefetch=1,
            grid=(n_redist, count),
            in_specs=[
                pl.BlockSpec((1, c_block, 1), lambda d, k, rep: (d * k_block + first + k, 0, 0)),
                pl.BlockSpec((1, virt), lambda d, k, rep: (0, 0)),
                pl.BlockSpec((1, c_block, j_slab, virt), source),
            ]
            + [pl.BlockSpec(hot.shape, lambda d, k, rep: (0, 0)) for hot in hots],
            out_specs=pl.BlockSpec((1, c_block, packed), lambda d, k, rep: (d * count + k, 0, 0)),
        ),
        compiler_params=pltpu.CompilerParams(vmem_limit_bytes=32 << 20),
        name="fold_integrals",
    )(rep_index[None], want, virt_irrep[None, :], integrals, *hots)


def fold_amps_kernel(width, want_ref, labels_ref, amps_ref, out_ref):
    virt = amps_ref.shape[2]
    zero = jnp.zeros((), jnp.float32)
    piece = 64
    for low in range(0, width, piece):
        total = None
        for start in range(low, virt, width):
            rows = slice(start, start + piece)
            keep = labels_ref[rows, :] == want_ref[0]
            part = jnp.where(keep, amps_ref[0, 0, rows, :].astype(jnp.float32), zero)
            total = part if total is None else total + part
        out_ref[0, 0, low : low + piece, :] = total.astype(out_ref.dtype)


def fold_amps(amplitudes, want, virt_irrep, width):
    i_slab, k_block, virt, _ = amplitudes.shape
    return pl.pallas_call(
        functools.partial(fold_amps_kernel, width),
        out_shape=jax.ShapeDtypeStruct((i_slab, k_block, width, virt), amplitudes.dtype),
        grid=(i_slab, k_block),
        in_specs=[
            pl.BlockSpec((1, 1, virt), lambda i, k: (k, 0, 0)),
            pl.BlockSpec((virt, 1), lambda i, k: (0, 0)),
            pl.BlockSpec((1, 1, virt, virt), lambda i, k: (i, k, 0, 0)),
        ],
        out_specs=pl.BlockSpec((1, 1, width, virt), lambda i, k: (i, k, 0, 0)),
        compiler_params=pltpu.CompilerParams(vmem_limit_bytes=32 << 20),
        cost_estimate=pl.CostEstimate(
            flops=2 * amplitudes.size, bytes_accessed=2 * amplitudes.size, transcendentals=0
        ),
        name="fold_amps",
    )(want, virt_irrep[:, None], amplitudes)


def contract_kernel(cuts, want_ref, labels_ref, amps_ref, ints_ref, *rest):
    hots, out_ref = rest[:-1], rest[-1]
    i_slab, _, width, virt = amps_ref.shape
    keep = want_ref[0] == labels_ref[...]
    amps = amps_ref[:, 0].reshape(i_slab * width, virt)
    k = pl.program_id(1)
    for j, (low, high, _) in enumerate(cuts):
        wide = jnp.dot(ints_ref[0, :, low:high], hots[j][...], preferred_element_type=jnp.float32)
        sym = jnp.where(keep, wide, 0.0).astype(jnp.bfloat16)
        part = jnp.dot(amps, sym, preferred_element_type=jnp.float32)

        for tile in range(out_ref.shape[0]):
            lanes = slice(tile * LANES, (tile + 1) * LANES)
            for i in range(i_slab):
                block = part[i * width : (i + 1) * width, lanes]

                @pl.when(k == 0)
                def _():
                    out_ref[tile, i, j] = block

                @pl.when(k > 0)
                def _():
                    out_ref[tile, i, j] += block


def contract(amps, moved, want, virt_irrep, cuts, width):
    i_slab, k_block, _, virt = amps.shape
    hots = [one_hot(virt, width, *cut).T for cut in cuts]
    step = min(virt, 512)
    return pl.pallas_call(
        functools.partial(contract_kernel, cuts),
        out_shape=jax.ShapeDtypeStruct(
            (virt // LANES, i_slab, len(cuts), width, LANES), jnp.float32
        ),
        grid=(virt // step, k_block),
        in_specs=[
            pl.BlockSpec((1, virt, 1), lambda n, k: (k, 0, 0)),
            pl.BlockSpec((1, step), lambda n, k: (0, n)),
            pl.BlockSpec((i_slab, 1, width, virt), lambda n, k: (0, k, 0, 0)),
            pl.BlockSpec((1, virt, moved.shape[2]), lambda n, k: (k, 0, 0)),
        ]
        + [pl.BlockSpec((hot.shape[0], step), lambda n, k: (0, n)) for hot in hots],
        out_specs=pl.BlockSpec(
            (step // LANES, i_slab, len(cuts), width, LANES), lambda n, k: (n, 0, 0, 0, 0)
        ),
        compiler_params=pltpu.CompilerParams(vmem_limit_bytes=48 << 20),
        name="contract",
    )(want, virt_irrep[None, :], amps, moved, *hots)


def body(amplitudes, integrals, occ_irrep, virt_irrep):
    n_redist = lax.axis_size("redist")
    n_rep = lax.axis_size("rep")
    dev_index = lax.axis_index("redist")
    rep_index = lax.axis_index("rep")
    i_slab, k_block, virt, _ = amplitudes.shape
    c_block = integrals.shape[1]
    j_slab = integrals.shape[2]
    b_block = virt // n_redist
    width = 3 * virt // 16
    slab_label = occ_irrep[0]

    k_labels = lax.dynamic_slice_in_dim(
        occ_irrep.reshape(n_redist, n_rep, k_block), rep_index, 1, 1
    ).reshape(n_redist * k_block)
    c_labels = lax.dynamic_slice_in_dim(virt_irrep, dev_index * c_block, c_block)
    want = k_labels[:, None] ^ c_labels[None, :] ^ slab_label
    sizes = (n_redist, n_rep, k_block)
    count = max(k_block // 2, 1)
    pieces = []
    for first in range(0, k_block, count):
        folded = fold_integrals(
            integrals, want[:, :, None], virt_irrep, rep_index, sizes, first, count, width
        )
        pieces.append(lax.all_to_all(folded, "redist", split_axis=0, concat_axis=1, tiled=True))
    moved = jnp.concatenate(pieces, axis=0)

    my_k = lax.dynamic_slice_in_dim(occ_irrep, (dev_index * n_rep + rep_index) * k_block, k_block)
    pair = my_k[:, None] ^ virt_irrep[None, :] ^ slab_label
    amps = fold_amps(amplitudes, pair[:, None, :], virt_irrep, width)

    part = contract(amps, moved, pair[:, :, None], virt_irrep, spans(j_slab, width), width)
    if b_block < LANES:
        part = part.reshape(*part.shape[:4], LANES // b_block, b_block)
        part = part.transpose(0, 4, 1, 2, 3, 5)
    part = part.reshape(n_redist * i_slab, j_slab, width, b_block)
    share = lax.psum_scatter(part, ("redist", "rep"), scatter_dimension=0, tiled=True)
    share = lax.all_gather(share, "rep", axis=0, tiled=True).transpose(0, 2, 1, 3)

    b_labels = lax.dynamic_slice_in_dim(virt_irrep, dev_index * b_block, b_block)
    out_keep = virt_irrep[:, None, None] == b_labels
    return jnp.where(out_keep, unfold(share, 1, virt), jnp.zeros((), jnp.float32))


def solution(mesh):
    placed = (P(None, ("redist", "rep"), None, None), P(None, "redist", None, None), P(), P())
    return jax.shard_map(
        body, mesh=mesh, in_specs=placed, out_specs=P(None, None, None, "redist"), check_vma=False
    )
```

time: 290 us -> 274 us (0.945)
  other arithmetic: 49.9 us -> 4.57 us
  blocking collectives: 0 us -> 18.8 us
  Pallas kernels: 82 us -> 92.2 us
  waiting for transfers between devices: 126 us -> 117 us
  local copies, waits for them, and re-layouts: 12.9 us -> 17.8 us
  starting transfers between devices: 5.6 us -> 9.51 us
    psum x1 -> x0, waiting for transfers between devices: 46.3 us -> none  [body(): shares.append(lax.psum(share, 'rep'))]
    reduce_scatter x2 -> x1, waiting for transfers between devices: 79.4 us -> 117 us  [body(): lax.psum_scatter(part, ('redist', 'rep'), scatter_dimension=0, tiled=True)]
    select_n x1 -> x0, other arithmetic: 24.2 us -> none  [body(): jnp.where(pair[:, None, :] == virt_irrep[None, :, None], amplitudes, zero)]
    all_gather x0 -> x1, blocking collectives: none -> 18.8 us  [body(): lax.all_gather(share, 'rep', axis=0, tiled=True).transpose(0, 2, 1, 3)]
    add x1 -> x0, other arithmetic: 15.2 us -> none  [fold(): total = piece if total is None else total + piece]
    pallas_call x2, Pallas kernels: 37.7 us -> 47.7 us  [the longest x1 28.2 us: contract(): pl.pallas_call(functools.partial(contract_kernel, cuts), out_shape=jax.Sh...]
    unnamed x10 -> x19, local copies, waits for them, and re-layouts: 0.7 us -> 6.07 us
    eq x1 -> x0, other arithmetic: 4.31 us -> none  [body(): pair[:, None, :] == virt_irrep[None, :, None]]
  transfers between devices with their start and end apart: 4 -> 3, of which waited for: 3 -> 1; matrix products, arithmetic and copies ran while one was open for 15% -> 1% of each run, Pallas kernels for 7% -> 15%
where the time goes in v3:
time: 274 us; the launch traced here: 273 us
  waiting for transfers between devices  117 us (43%)
  Pallas kernels  92.2 us (34%)
  blocking collectives  18.8 us (7%)
  local copies, waits for them, and re-layouts  17.8 us (6%)
  between operations  13.6 us (5%)
  starting transfers between devices  9.51 us (3%)
  other arithmetic  4.57 us (2%)
    reduce_scatter x1, waiting for transfers between devices, body(): lax.psum_scatter(part, ('redist', 'rep'), scatter_dimension=0, tiled=True)  117 us
    pallas_call x2, Pallas kernels, fold_integrals(): pl.pallas_call(functools.partial(fold_kernel, cuts), out_shape=jax.ShapeD...  44.6 us
    pallas_call x1, Pallas kernels, contract(): pl.pallas_call(functools.partial(contract_kernel, cuts), out_shape=jax.Sh...  28.2 us
    pallas_call x1, Pallas kernels, fold_amps(): pl.pallas_call(functools.partial(fold_amps_kernel, width), out_shape=jax....  19.4 us
    all_gather x1, blocking collectives, body(): lax.all_gather(share, 'rep', axis=0, tiled=True).transpose(0, 2, 1, 3)  18.8 us
    all_to_all x2, starting transfers between devices, body(): lax.all_to_all(folded, 'redist', split_axis=0, concat_axis=1, tiled=True)  9.47 us
    unnamed x19, local copies, waits for them, and re-layouts  6.07 us
  transfers between devices with their start and end apart: 3, of which 1 were waited for; matrix products, arithmetic and copies ran while one was open for 1% of the time, Pallas kernels for 15%

profile of v3, /device:TPU:0, one launch (start us, length us, event | category | flops | bytes accessed | tf_op | source)
XLA Modules:
  0.0 273.2 jit_solution(1803253108034029323)
XLA Ops:
  6.6 0.8 reshape.171
  7.4 0.1 xor.102
  7.4 0.8 dynamic_slice.10
  8.2 0.3 fusion
  8.5 1.0 xor_xor_fusion.want_ref
  9.6 0.7 copy-done.3
  10.2 22.2 %fold_integrals.2 = bf16[16,128,384]{2,1,0:T(8,128)(2,1)S(1)} custom-call(s32[1]{0:T(128)} %bitcast.3._, s32[32,128,1]{2,1,0:T(8,128)S(1)} %xor_xor_fusion.want_ref, s32[1,1024]{1,0:T(1,128)S(1)} %bitcast.21, bf16[128,128,2,1024]{3,2,1,0:T(2,128)(2,1)} %ints_ref.3, bf16[1024,256]{1,0:T(8,128)(2,1)S(1)} %get-tuple-element.5.rest_0_, ...), custom_call_target="tpu_custom_call" | custom-call | tf_op jit(solution)/shard_map/fold_integrals/pallas_call | solution.py:58
  32.5 1.1 copy-done.2
  33.6 5.2 %all-to-all-start = ((bf16[16,128,384]{2,1,0:T(8,128)(2,1)}), bf16[16,128,384]{2,1,0:T(8,128)(2,1)}, u32[]{:S(2)}, u32[]{:S(2)}) async-start(bf16[16,128,384]{2,1,0:T(8,128)(2,1)} %copy-done.2), calls=%async_computation | async-start | bytes 3145728 | tf_op jit(solution)/shard_map/all_to_all | solution.py:185
  38.8 22.3 %fold_integrals.3 = bf16[16,128,384]{2,1,0:T(8,128)(2,1)S(1)} custom-call(s32[1]{0:T(128)} %bitcast.3._, s32[32,128,1]{2,1,0:T(8,128)S(1)} %xor_xor_fusion.want_ref, s32[1,1024]{1,0:T(1,128)S(1)} %bitcast.22, bf16[128,128,2,1024]{3,2,1,0:T(2,128)(2,1)} %ints_ref.3, bf16[1024,256]{1,0:T(8,128)(2,1)S(1)} %get-tuple-element.5.rest_0_, ...), custom_call_target="tpu_custom_call" | custom-call | tf_op jit(solution)/shard_map/fold_integrals/pallas_call | solution.py:58
  61.2 1.1 copy-done.1
  62.3 4.3 %all-to-all-start.1 = ((bf16[16,128,384]{2,1,0:T(8,128)(2,1)}), bf16[16,128,384]{2,1,0:T(8,128)(2,1)}, u32[]{:S(2)}, u32[]{:S(2)}) async-start(bf16[16,128,384]{2,1,0:T(8,128)(2,1)} %copy-done.1), calls=%async_computation.1 | async-start | bytes 3145728 | tf_op jit(solution)/shard_map/all_to_all | solution.py:185
  66.7 0.1 dynamic_slice.11
  66.8 0.2 copy.18.labels_ref
  67.0 0.1 xor_xor_fusion.2.want_ref
  67.1 19.4 %fold_amps.1.amps_ref = bf16[4,4,192,1024]{3,2,1,0:T(8,128)(2,1)S(1)} custom-call(s32[4,1,1024]{2,1,0:T(1,128)S(1)} %xor_xor_fusion.2.want_ref, s32[1024,1]{1,0:T(8,128)S(1)} %copy.18.labels_ref, bf16[4,4,1024,1024]{3,2,1,0:T(8,128)(2,1)} %amps_ref.1), custom_call_target="tpu_custom_call" | custom-call | flops 33554432 | bytes 33554432 | tf_op jit(solution)/shard_map/fold_amps/pallas_call | solution.py:93
  86.6 2.7 copy-done
  89.2 0.3 fusion.2
  89.5 0.3 xor_xor_fusion.1.want_ref
  89.8 2.8 %copy.19 = bf16[8,2,128,384]{3,2,0,1:T(8,128)(2,1)} copy(bf16[8,2,128,384]{3,2,1,0:T(8,128)(2,1)} %bitcast.4) | data formatting | bytes 3145728 | tf_op jit(solution)/shard_map/all_to_all | solution.py:185
  92.5 1.7 copy.20
  94.3 0.2 copy-done.5
  94.4 2.0 pad_maximum_fusion.ints_ref
  96.4 28.2 %contract.1 = f32[8,4,2,192,128]{4,3,2,1,0:T(8,128)} custom-call(s32[4,1024,1]{2,1,0:T(8,128)S(1)} %xor_xor_fusion.1.want_ref, s32[1,1024]{1,0:T(1,128)S(1)} %bitcast.24, bf16[4,4,192,1024]{3,2,1,0:T(8,128)(2,1)} %copy-done, bf16[4,1024,384]{2,1,0:T(8,128)(2,1)} %pad_maximum_fusion.ints_ref, bf16[256,1024]{1,0:T(8,128)(2,1)S(1)} %get-tuple-element.7.rest_0_, ...), custom_call_target="tpu_custom_call" | custom-call | tf_op jit(solution)/shard_map/contract/pallas_call | solution.py:140
  124.7 0.2 broadcast_compare_fusion
  124.9 116.7 %reduce-scatter.2.cloned.1.call-done = f32[1,2,192,128]{3,2,1,0:T(8,128)} async-done(((f32[32,2,192,128]{3,2,1,0:T(8,128)}), f32[1,2,192,128]{3,2,1,0:T(8,128)}) %reduce-scatter.2.cloned.1.call-update) | async-done | bytes 196624 | tf_op jit(solution)/shard_map/reduce_scatter | solution.py:197
  241.6 18.8 %all_gather.3 = f32[4,2,192,128]{3,2,1,0:T(8,128)S(1)} all-gather(f32[1,2,192,128]{3,2,1,0:T(8,128)} %reduce-scatter.2.cloned.1.call-done), channel_id=1, replica_groups=mesh['redist'=8,'rep'=4] {'rep'}, dimensions={0}, use_global_device_ids=true | all-gather | bytes 983040 | tf_op jit(solution)/shard_map/all_gather | solution.py:198
  260.5 0.1 bitcast_dynamic-update-slice_fusion.3
  260.5 0.1 bitcast_dynamic-update-slice_fusion.2
  260.7 0.1 bitcast_dynamic-update-slice_fusion.5
  260.8 0.3 slice_select_fusion
  261.1 5.2 %copy.21 = f32[4,1024,2,128]{3,2,1,0:T(2,128)} copy(f32[4,1024,2,128]{3,1,2,0:T(8,128)S(1)} %slice_select_fusion) | data formatting | bytes 8388608 | tf_op jit(solution)/shard_map/jit(_where)/select_n | solution.py:202
  (19 shorter events, 0.3 us)
Async XLA Ops:
  9.5 0.7 copy-start.3
  10.2 28.6 %copy-start.4 = (s32[1024]{0:T(1024)S(1)}, s32[1024]{0:T(1024)}, u32[]{:S(2)}) copy-start(s32[1024]{0:T(1024)} %param.7) | copy-start | bytes 12292
  32.5 1.2 copy-start.2
  33.6 28.7 %all-to-all-start = ((bf16[16,128,384]{2,1,0:T(8,128)(2,1)}), bf16[16,128,384]{2,1,0:T(8,128)(2,1)}, u32[]{:S(2)}, u32[]{:S(2)}) async-start(bf16[16,128,384]{2,1,0:T(8,128)(2,1)} %copy-done.2), calls=%async_computation | async-start | bytes 3145728 | tf_op jit(solution)/shard_map/all_to_all | solution.py:185
  38.8 27.9 %copy-start.6 = (s32[128]{0:T(128)S(1)}, s32[128]{0:T(128)}, u32[]{:S(2)}) copy-start(s32[128]{0:T(128)} %param.6) | copy-start | bytes 1540
  61.1 1.1 copy-start.1
  62.3 30.2 %all-to-all-start.1 = ((bf16[16,128,384]{2,1,0:T(8,128)(2,1)}), bf16[16,128,384]{2,1,0:T(8,128)(2,1)}, u32[]{:S(2)}, u32[]{:S(2)}) async-start(bf16[16,128,384]{2,1,0:T(8,128)(2,1)} %copy-done.1), calls=%async_computation.1 | async-start | bytes 3145728 | tf_op jit(solution)/shard_map/all_to_all | solution.py:185
  66.6 175.0 %reduce-scatter.2.cloned.1.call-start = ((), (), s32[]{:S(2)}) async-start(), calls=%async_computation.3 | async-start | bytes 6488064 | tf_op jit(solution)/shard_map/reduce_scatter | solution.py:197
  86.5 2.7 copy-start
  92.5 1.9 copy-start.5
Sparse Core Ops, SparseCore 0:
  124.8 116.7 reduce-scatter.1
